TPU v7x, 32 devices: a whole 2x2x4 slice. The times are simulated.
32 devices in a mesh: member: 2 (over x), grid: 16 (over z, y, core).
Axes of the slice: x: 2, y: 2, z: 4, core: 2. Of those that a mesh axis runs over, the one named last changes fastest.
Arguments:
- states: bfloat16 [2, 2048, 1024], P('member', 'grid'), may hold values from -6 to 6
- norm_scale_vector: float32 [1024], replicated, may hold values from 0.1 to 1.9
- query_weight: bfloat16 [1024, 512], P('grid'), may hold values from -2 to 2
- key_weight: bfloat16 [1024, 512], P('grid'), may hold values from -2 to 2
- value_weight: bfloat16 [1024, 512], P('grid'), may hold values from -0.1875 to 0.1875
- output_weight: bfloat16 [512, 1024], P('grid'), may hold values from -0.25 to 0.25
- head_weight: bfloat16 [1024, 128], P('grid'), may hold values from -0.5 to 0.5
- neighbours: int32 [2048, 8], P('grid'), may hold values from 0 to 2047, as said below
- observed: float32 [2048, 128], P('grid'), may hold values from -16 to 16
Outputs:
- grad_input: bfloat16 [2, 2048, 1024], P('member', 'grid')
- grad_mixing: float32 [512, 1024], P('grid')
- grad_head: float32 [1024, 128], P('grid')
- grad_key_value: float32 [2, 2048, 1024], P('member', 'grid')
Inputs may be any that keep to these rules, and one draw needn't show every extreme that they name: `neighbours`: the first neighbour of every point is the point itself; every neighbour index lies within 32 positions of the point's own index, and that distance occurs.
All inputs are finite; a program needn't handle non-finite values.
Results may differ from a plain program's by a relative error of at most 0.035.
Values may be sent and summed in bfloat16 or wider, within the bound.
A program may use at most 64 MiB of HBM per device.

v0:
```python
import math

import jax
import jax.numpy as jnp
from jax import lax
from jax.sharding import PartitionSpec as P

HEADS = 8
HDIM = 64
KNB = 8
HALO = 32


epsilon = 1e-05
smooth = 0.1


def extended_2(x, sides, width):
    for axis, dim in sides:
        devices, length = (lax.axis_size(axis), x.shape[dim])
        up = [(i, (i + 1) % devices) for i in range(devices - 1)]
        down = [(j, i) for i, j in up]
        last = lax.slice_in_dim(x, length - width, length, axis=dim)
        leading = lax.slice_in_dim(x, 0, width, axis=dim)
        before = lax.ppermute(last, axis, up)
        after = lax.ppermute(leading, axis, down)
        x = jnp.concatenate([before, x, after], axis=dim)
    return x


def passed_along(block, axis, distance):
    devices = range(lax.axis_size(axis))
    route = [(i - distance, i) for i in devices if i - distance in devices]
    return lax.ppermute(block, axis, route)


def layer_norm(states):
    values = states.astype(jnp.float32)
    center = values - jnp.mean(values, axis=-1, keepdims=True)
    inverse_spread = lax.rsqrt(jnp.mean(center * center, axis=-1, keepdims=True) + epsilon)
    return (center * inverse_spread, inverse_spread)


def gradient_of(spread):
    return spread / jnp.sqrt(spread * spread + smooth * smooth)


def attend(query_rows, gathered):
    number = query_rows.shape[0]
    inner_width = query_rows.shape[1]
    query_heads = query_rows.reshape(number, HEADS, HDIM)
    key_heads = gathered[:, :, :inner_width].reshape(number, KNB, HEADS, HDIM)
    value_heads = gathered[:, :, inner_width:].reshape(number, KNB, HEADS, HDIM)
    scores = jnp.einsum(
        "rhe,rkhe->rhk", query_heads, key_heads, preferred_element_type=jnp.float32
    ) * (1.0 / math.sqrt(HDIM))
    highest = jnp.max(scores, axis=-1, keepdims=True)
    exponent = jnp.exp(scores - highest)
    attention = exponent / jnp.sum(exponent, axis=-1, keepdims=True)
    attention_cast = attention.astype(jnp.bfloat16)
    attended_rows = jnp.einsum(
        "rhk,rkhe->rhe", attention_cast, value_heads, preferred_element_type=jnp.float32
    )
    return (
        attended_rows.reshape(number, inner_width).astype(jnp.bfloat16),
        attention,
        attention_cast,
    )


def attend_back(query_rows, gathered, attention, attention_cast, grad_mixed):
    number = query_rows.shape[0]
    inner_width = query_rows.shape[1]
    query_heads = query_rows.reshape(number, HEADS, HDIM)
    key_heads = gathered[:, :, :inner_width].reshape(number, KNB, HEADS, HDIM)
    value_heads = gathered[:, :, inner_width:].reshape(number, KNB, HEADS, HDIM)
    grad_heads = grad_mixed.reshape(number, HEADS, HDIM)
    grad_prob = jnp.einsum(
        "rhe,rkhe->rhk", grad_heads, value_heads, preferred_element_type=jnp.float32
    )
    grad_score = (
        attention
        * (grad_prob - jnp.sum(attention * grad_prob, axis=-1, keepdims=True))
        * (1.0 / math.sqrt(HDIM))
    )
    grad_query = jnp.einsum(
        "rhk,rkhe->rhe", grad_score, key_heads, preferred_element_type=jnp.float32
    )
    grad_keys = jnp.einsum(
        "rhk,rhe->rkhe", grad_score, query_heads, preferred_element_type=jnp.float32
    )
    grad_values = jnp.einsum(
        "rhk,rhe->rkhe", attention_cast, grad_heads, preferred_element_type=jnp.float32
    )
    returned = jnp.concatenate(
        [
            grad_keys.reshape(number, KNB, inner_width),
            grad_values.reshape(number, KNB, inner_width),
        ],
        axis=-1,
    )
    return (grad_query.reshape(number, inner_width).astype(jnp.bfloat16), returned)


def transposed(left, right):
    return lax.dot_general(
        left, right, (((1,), (1,)), ((), ())), preferred_element_type=jnp.float32
    )


def shards(
    states,
    norm_scale_vector,
    query_weight,
    key_weight,
    value_weight,
    output_weight,
    head_weight,
    neighbours,
    observed,
):
    points = states.shape[1]
    inner_width = query_weight.shape[1]
    inputs = states[0]
    centred_rows, inverse_spread = layer_norm(inputs)
    normed = (centred_rows * norm_scale_vector).astype(jnp.bfloat16)
    full_query, full_key, full_value = (
        lax.all_gather(query_weight, "grid", axis=0, tiled=True),
        lax.all_gather(key_weight, "grid", axis=0, tiled=True),
        lax.all_gather(value_weight, "grid", axis=0, tiled=True),
    )
    query_rows = jnp.dot(normed, full_query, preferred_element_type=jnp.float32).astype(
        jnp.bfloat16
    )
    key_part = jnp.dot(normed, full_key, preferred_element_type=jnp.float32)
    value_part = jnp.dot(normed, full_value, preferred_element_type=jnp.float32)
    key_value_pair = jnp.concatenate(
        [key_part.astype(jnp.bfloat16), value_part.astype(jnp.bfloat16)], axis=1
    )
    extended = extended_2(key_value_pair, (("grid", 0),), HALO)
    local_rows = neighbours - (lax.axis_index("grid") * points - HALO)
    gathered = jnp.take(extended, local_rows, axis=0)
    attended_rows, attention, attention_cast = attend(query_rows, gathered)
    residual = inputs.astype(jnp.float32)
    full_out = lax.all_gather(output_weight, "grid", axis=0, tiled=True)
    layer_output = (
        residual + jnp.dot(attended_rows, full_out, preferred_element_type=jnp.float32)
    ).astype(jnp.bfloat16)
    complete_head = lax.all_gather(head_weight, "grid", axis=0, tiled=True)
    member_prediction = jnp.dot(layer_output, complete_head, preferred_element_type=jnp.float32)
    member_list = lax.axis_size("member")
    every_member = lax.all_gather(member_prediction[None], "member", axis=0, tiled=True)
    pairwise_total = jnp.sum(gradient_of(member_prediction[None] - every_member), axis=0)
    prediction_gradient = (
        gradient_of(member_prediction - observed) - pairwise_total / (member_list - 1)
    ).astype(jnp.bfloat16)
    back_head = lax.all_gather(head_weight, "grid", axis=0, tiled=True)
    grad_output = transposed(prediction_gradient, back_head)
    output_cast = grad_output.astype(jnp.bfloat16)
    back_out = lax.all_gather(output_weight, "grid", axis=0, tiled=True)
    grad_mixed = transposed(output_cast, back_out).astype(jnp.bfloat16)
    grad_query, returned = attend_back(query_rows, gathered, attention, attention_cast, grad_mixed)
    margin = HALO
    summed = jax.ops.segment_sum(
        returned.reshape(points * KNB, 2 * inner_width),
        local_rows.reshape(points * KNB),
        num_segments=points + 2 * margin,
    )
    lower = summed[:margin]
    upper = summed[points + margin :]
    middle = summed[margin : points + margin]
    from_after = passed_along(lower.astype(jnp.bfloat16), "grid", -1).astype(lower.dtype)
    from_before = passed_along(upper.astype(jnp.bfloat16), "grid", 1).astype(upper.dtype)
    middle = middle.at[:margin].add(from_before)
    middle = middle.at[points - margin :].add(from_after)
    grad_keys = middle[:, :inner_width].astype(jnp.bfloat16)
    grad_values = middle[:, inner_width:].astype(jnp.bfloat16)
    back_query, back_key, back_value = (
        lax.all_gather(query_weight, "grid", axis=0, tiled=True),
        lax.all_gather(key_weight, "grid", axis=0, tiled=True),
        lax.all_gather(value_weight, "grid", axis=0, tiled=True),
    )
    grad_normed = transposed(grad_query, back_query)
    grad_normed = grad_normed + transposed(grad_keys, back_key)
    grad_normed = grad_normed + transposed(grad_values, back_value)
    grad_centred = grad_normed * norm_scale_vector
    grad_states = inverse_spread * (
        grad_centred
        - jnp.mean(grad_centred, axis=-1, keepdims=True)
        - centred_rows * jnp.mean(grad_centred * centred_rows, axis=-1, keepdims=True)
    )
    grad_input = (grad_output + grad_states).astype(jnp.bfloat16)[None]
    columns = attended_rows.astype(jnp.float32)
    mixing_share = lax.psum_scatter(
        lax.dot_general(
            columns, grad_output, (((0,), (0,)), ((), ())), precision=lax.Precision.HIGHEST
        ),
        "grid",
        scatter_dimension=0,
        tiled=True,
    )
    columns = layer_output
    head_share = lax.psum_scatter(
        lax.dot_general(
            columns,
            prediction_gradient,
            (((0,), (0,)), ((), ())),
            preferred_element_type=jnp.float32,
        ),
        "grid",
        scatter_dimension=0,
        tiled=True,
    )
    mixing_total, head_total = (
        lax.psum(mixing_share.astype(jnp.bfloat16), "member").astype(jnp.float32),
        lax.psum(head_share.astype(jnp.bfloat16), "member").astype(jnp.float32),
    )
    scaling = 1.0 / math.sqrt(member_list * lax.axis_size("grid") * points)
    return (grad_input, mixing_total * scaling, head_total * scaling, middle[None])


def solution(mesh):
    return jax.shard_map(
        shards,
        mesh=mesh,
        in_specs=(
            P("member", "grid", None),
            P(),
            P("grid", None),
            P("grid", None),
            P("grid", None),
            P("grid", None),
            P("grid", None),
            P("grid", None),
            P("grid", None),
        ),
        out_specs=(
            P("member", "grid", None),
            P("grid", None),
            P("grid", None),
            P("member", "grid", None),
        ),
        check_vma=False,
    )
```

profile of v0, /device:TPU:0, one launch (start us, length us, event | category | flops | bytes accessed | tf_op | source)
XLA Modules:
  0.0 326.8 jit_solution(9513562597920504864)
XLA Ops:
  13.4 25.1 %all_gather.27 = bf16[1024,128]{1,0:T(8,128)(2,1)S(1)} all-gather(bf16[64,128]{1,0:T(8,128)(2,1)} %param.19), channel_id=1, replica_groups=mesh['member'=2,'grid'=16] {'grid'}, dimensions={0}, use_global_device_ids=true | all-gather | bytes 278528 | tf_op jit(solution)/shard_map/all_gather | solution.py:149
  38.5 12.6 %all-gather.6.cloned.1.call-done = bf16[1024,512]{1,0:T(8,128)(2,1)} async-done(((bf16[64,512]{1,0:T(8,128)(2,1)}), bf16[1024,512]{1,0:T(8,128)(2,1)}) %all-gather.6.cloned.1.call-update) | async-done | bytes 1048592 | tf_op jit(solution)/shard_map/all_gather | solution.py:128
  52.9 37.2 %all-gather.8.cloned.1.call-done = bf16[1024,512]{1,0:T(8,128)(2,1)} async-done(((bf16[64,512]{1,0:T(8,128)(2,1)}), bf16[1024,512]{1,0:T(8,128)(2,1)}) %all-gather.8.cloned.1.call-update) | async-done | bytes 1048592 | tf_op jit(solution)/shard_map/all_gather | solution.py:129
  91.7 37.5 %all-gather.10.cloned.1.call-done = bf16[1024,512]{1,0:T(8,128)(2,1)} async-done(((bf16[64,512]{1,0:T(8,128)(2,1)}), bf16[1024,512]{1,0:T(8,128)(2,1)}) %all-gather.10.cloned.1.call-update) | async-done | bytes 1048592 | tf_op jit(solution)/shard_map/all_gather | solution.py:130
  130.8 2.2 collective-permute-start
  136.2 4.1 %gather_fusion = bf16[1024,1024]{1,0:T(8,128)(2,1)S(1)} fusion(bf16[192,1024]{1,0:T(8,128)(2,1)S(1)} %pad_maximum_fusion, s32[1024]{0:T(1024)S(1)} %broadcast_clamp_fusion), kind=kCustom, calls=%fused_computation | custom fusion | bytes 4198400 | tf_op jit(solution)/shard_map/jit(_take)/gather | solution.py:142
  140.2 2.9 copy.16
  143.1 1.8 broadcast_select_fusion
  144.9 1.7 multiply_reduce_fusion.3
  148.6 19.6 %all-gather.12.cloned.1.call-done = bf16[512,1024]{1,0:T(8,128)(2,1)} async-done(((bf16[32,1024]{1,0:T(8,128)(2,1)}), bf16[512,1024]{1,0:T(8,128)(2,1)}) %all-gather.12.cloned.1.call-update) | async-done | bytes 1048592 | tf_op jit(solution)/shard_map/all_gather | solution.py:145
  169.9 4.9 %all-gather = f32[256,128]{1,0:T(8,128)S(1)} all-gather(f32[128,128]{1,0:T(8,128)S(1)} %fusion.50), channel_id=2, replica_groups=mesh['member'=2,'grid'=16] {'member'}, dimensions={0}, use_global_device_ids=true | all-gather | bytes 196608 | tf_op jit(solution)/shard_map/all_gather | solution.py:152
  176.3 1.7 convolution_convert_fusion
  179.8 2.3 fusion.53
  182.4 2.8 fusion.13
  185.4 3.1 multiply_bitcast_fusion.1
  188.5 3.5 %concatenate.20 = f32[1024,512]{1,0:T(8,128)S(1)} reshape(f32[128,8,8,64]{3,2,1,0:T(8,128)} %multiply_bitcast_fusion.1) | data formatting | bytes 4194304 | tf_op jit(solution)/shard_map/concatenate | solution.py:95
  192.0 4.1 %multiply_bitcast_fusion = f32[128,8,8,64]{3,2,1,0:T(8,128)} fusion(f32[128,8,8]{1,2,0:T(8,128)S(1)} %copy-done.8, f32[128,8,64]{2,1,0:T(8,128)} %copy.20), kind=kLoop, calls=%fused_computation.9 | loop fusion | flops 524288 | bytes 2392064 | tf_op jit(solution)/shard_map/rhk,rhe->rkhe/transpose | solution.py:92
  196.1 4.8 %concatenate.21 = f32[1024,512]{1,0:T(8,128)} reshape(f32[128,8,8,64]{3,2,1,0:T(8,128)} %multiply_bitcast_fusion) | data formatting | bytes 4194304 | tf_op jit(solution)/shard_map/concatenate | solution.py:95
  200.9 10.6 %scatter_custom_fusion = f32[192,1024]{1,0:T(8,128)} fusion(s32[1024]{0:T(1024)S(1)} %reshape.128, f32[1024,512]{1,0:T(8,128)} %concatenate.21, f32[]{:T(128)} %constant.98.clone.1, f32[1024,512]{1,0:T(8,128)S(1)} %concatenate.20, f32[]{:T(128)} %constant.87.clone.1), kind=kCustom, calls=%fused_computation.5 | custom fusion | flops 2097152 | bytes 4980744 | tf_op jit(solution)/shard_map/scatter-add | solution.py:164
  214.3 3.0 collective-permute-start.2
  221.2 9.9 %reduce-scatter.5.cloned.1.call-done = f32[64,128]{1,0:T(8,128)} async-done(((f32[1024,128]{1,0:T(8,128)}), f32[64,128]{1,0:T(8,128)}) %reduce-scatter.5.cloned.1.call-update) | async-done | bytes 32784 | tf_op jit(solution)/shard_map/reduce_scatter | solution.py:203
  231.9 8.1 %psum.15 = bf16[64,128]{1,0:T(8,128)(2,1)S(1)} all-reduce(bf16[64,128]{1,0:T(8,128)(2,1)S(1)} %convert_element_type.92), channel_id=1, replica_groups=mesh['member'=2,'grid'=16] {'member'}, use_global_device_ids=true, to_apply=%region_12.13 | all-reduce | flops 8192 | bytes 32768 | tf_op jit(solution)/shard_map/psum | solution.py:216
  240.0 55.8 %reduce-scatter.3.cloned.1.call-done = f32[32,1024]{1,0:T(8,128)} async-done(((f32[512,1024]{1,0:T(8,128)}), f32[32,1024]{1,0:T(8,128)}) %reduce-scatter.3.cloned.1.call-update) | async-done | bytes 131088 | tf_op jit(solution)/shard_map/reduce_scatter | solution.py:194
  298.0 20.4 %all-reduce.2.cloned.1.call-done = bf16[32,1024]{1,0:T(8,128)(2,1)} async-done(((bf16[32,1024]{1,0:T(8,128)(2,1)}), bf16[32,1024]{1,0:T(8,128)(2,1)}) %all-reduce.2.cloned.1.call-update) | async-done | bytes 65552 | tf_op jit(solution)/shard_map/psum | solution.py:215
  (104 shorter events, 32.5 us)
Async XLA Ops:
  7.2 83.0 %copy-start.2 = (bf16[1,128,1024]{2,1,0:T(8,128)(2,1)S(1)}, bf16[1,128,1024]{2,1,0:T(8,128)(2,1)}, u32[]{:S(2)}) copy-start(bf16[1,128,1024]{2,1,0:T(8,128)(2,1)} %param.13) | copy-start | bytes 786436
  7.2 83.0 %copy-start.14 = (f32[1024]{0:T(1024)S(1)}, f32[1024]{0:T(1024)}, u32[]{:S(2)}) copy-start(f32[1024]{0:T(1024)} %param.14) | copy-start | bytes 12292
  7.2 43.9 %all-gather.6.cloned.1.call-start = ((), (), s32[]{:S(2)}) async-start(), calls=%async_computation.2 | async-start | bytes 1114112 | tf_op jit(solution)/shard_map/all_gather | solution.py:128
  7.9 82.2 %all-gather.8.cloned.1.call-start = ((), (), s32[]{:S(2)}) async-start(), calls=%async_computation.3 | async-start | bytes 1114112 | tf_op jit(solution)/shard_map/all_gather | solution.py:129
  8.7 120.5 %all-gather.10.cloned.1.call-start = ((), (), s32[]{:S(2)}) async-start(), calls=%async_computation.4 | async-start | bytes 1114112 | tf_op jit(solution)/shard_map/all_gather | solution.py:130
  9.4 158.7 %all-gather.12.cloned.1.call-start = ((), (), s32[]{:S(2)}) async-start(), calls=%async_computation.5 | async-start | bytes 1114112 | tf_op jit(solution)/shard_map/all_gather | solution.py:145
  10.0 221.2 %reduce-scatter.5.cloned.1.call-start = ((), (), s32[]{:S(2)}) async-start(), calls=%async_computation.8 | async-start | bytes 557056 | tf_op jit(solution)/shard_map/reduce_scatter | solution.py:203
  130.8 4.5 %collective-permute-start = (bf16[32,1024]{1,0:T(8,128)(2,1)S(1)}, bf16[32,1024]{1,0:T(8,128)(2,1)S(1)}, u32[]{:S(2)}, u32[]{:S(2)}) collective-permute-start(bf16[32,1024]{1,0:T(8,128)(2,1)S(1)} %get-tuple-element.36), channel_id=1, source_target_pairs={{0,1},{1,2},{2,3},{3,4},{4,5},{5,6},{6,7},{7,8},{8,9},{9,10},{10,1... | collective-permute-start | bytes 196616 | tf_op jit(solution)/shard_map/ppermute | solution.py:25
  133.0 3.1 collective-permute-start.1
  148.1 26.8 %copy-start.7 = (f32[128,8,8]{1,2,0:T(8,128)}, f32[128,8,8]{1,2,0:T(8,128)S(1)}, u32[]{:S(2)}) copy-start(f32[128,8,8]{1,2,0:T(8,128)S(1)} %get-tuple-element.38) | copy-start | bytes 98308
  148.3 26.6 %copy-start.13 = (f32[128,128]{1,0:T(8,128)S(1)}, f32[128,128]{1,0:T(8,128)}, u32[]{:S(2)}) copy-start(f32[128,128]{1,0:T(8,128)} %param.21) | copy-start | bytes 196612
  175.2 4.1 %copy-start.1 = (bf16[128,8,1024]{0,2,1:T(8,128)(2,1)S(1)}, bf16[128,8,1024]{0,2,1:T(8,128)(2,1)}, u32[]{:S(2)}) copy-start(bf16[128,8,1024]{0,2,1:T(8,128)(2,1)} %copy-done) | copy-start | bytes 6291460
  176.3 119.5 %reduce-scatter.3.cloned.1.call-start = ((), (), s32[]{:S(2)}) async-start(), calls=%async_computation.6 | async-start | bytes 2228224 | tf_op jit(solution)/shard_map/reduce_scatter | solution.py:194
  179.8 2.6 copy-start.12
  182.2 3.2 copy-start.6
  182.2 136.3 %all-reduce.2.cloned.1.call-start = ((), (), s32[]{:S(2)}) async-start(), calls=%async_computation.7 | async-start | bytes 131072 | tf_op jit(solution)/shard_map/psum | solution.py:215
  188.5 3.5 %copy-start.8 = (f32[128,8,8]{1,2,0:T(8,128)S(1)}, f32[128,8,8]{1,2,0:T(8,128)}, u32[]{:S(2)}) copy-start(f32[128,8,8]{1,2,0:T(8,128)} %copy-done.7) | copy-start | bytes 98308
  211.5 5.9 %copy-start.5 = (bf16[128,8,512]{0,2,1:T(8,128)(2,1)S(1)}, bf16[128,8,512]{0,2,1:T(8,128)(2,1)}, u32[]{:S(2)}) copy-start(bf16[128,8,512]{0,2,1:T(8,128)(2,1)} %get-tuple-element.31) | copy-start | bytes 3145732
  211.5 6.1 %copy-start.11 = (bf16[1024,512]{1,0:T(8,128)(2,1)S(1)}, bf16[1024,512]{1,0:T(8,128)(2,1)}, u32[]{:S(2)}) copy-start(bf16[1024,512]{1,0:T(8,128)(2,1)} %all-gather.6.cloned.1.call-done) | copy-start | bytes 3145732
  212.8 5.4 %copy-start.3 = (f32[192,1024]{1,0:T(8,128)S(1)}, f32[192,1024]{1,0:T(8,128)}, u32[]{:S(2)}) copy-start(f32[192,1024]{1,0:T(8,128)} %scatter_custom_fusion) | copy-start | bytes 2359300
  212.8 5.4 %slice-start.1 = ((f32[192,1024]{1,0:T(8,128)}), f32[128,1024]{1,0:T(8,128)S(1)}, s32[]{:S(2)}) async-start(f32[192,1024]{1,0:T(8,128)} %scatter_custom_fusion), calls=%async_computation.10 | async-start | bytes 1048576 | tf_op jit(solution)/shard_map/slice | solution.py:171
  212.9 5.4 %collective-permute-start.3 = (bf16[32,1024]{1,0:T(8,128)(2,1)S(1)}, bf16[32,1024]{1,0:T(8,128)(2,1)S(1)}, u32[]{:S(2)}, u32[]{:S(2)}) collective-permute-start(bf16[32,1024]{1,0:T(8,128)(2,1)S(1)} %get-tuple-element.34), channel_id=1, source_target_pairs={{1,0},{2,1},{3,2},{4,3},{5,4},{6,5},{7,6},{8,7},{9,8},{10,9},{11,1... | collective-permute-start | bytes 196616 | tf_op jit(solution)/shard_map/ppermute | solution.py:34
  214.3 3.9 %collective-permute-start.2 = (bf16[32,1024]{1,0:T(8,128)(2,1)S(1)}, bf16[32,1024]{1,0:T(8,128)(2,1)S(1)}, u32[]{:S(2)}, u32[]{:S(2)}) collective-permute-start(bf16[32,1024]{1,0:T(8,128)(2,1)S(1)} %get-tuple-element.35), channel_id=1, source_target_pairs={{0,1},{1,2},{2,3},{3,4},{4,5},{5,6},{6,7},{7,8},{8,9},{9,10},{10,1... | collective-permute-start | bytes 196616 | tf_op jit(solution)/shard_map/ppermute | solution.py:34
  218.3 1.9 copy-start.4
  (4 other events, 6.1 us)
Sparse Core Ops, SparseCore 0:
  10.2 40.8 all-gather.5
  53.3 36.8 all-gather.7
  92.3 36.8 all-gather.9
  131.2 36.8 all-gather.11
  176.4 54.6 reduce-scatter.4
  235.2 60.5 reduce-scatter.2
  298.6 19.7 all-reduce.1
where the time goes:
time: 328 us; the launch traced here: 327 us
  waiting for transfers between devices  197 us (60%)
  blocking collectives  38.1 us (12%)
  other arithmetic  36 us (11%)
  local copies, waits for them, and re-layouts  19.6 us (6%)
  between operations  14.6 us (4%)
  matrix products  13.5 us (4%)
  starting transfers between devices  8.37 us (3%)
    reduce_scatter x1, waiting for transfers between devices, shards(): lax.psum_scatter(lax.dot_general(columns, grad_output, (((0,), (0,)), (()...  55.8 us
    all_gather x1, waiting for transfers between devices, shards(): lax.all_gather(value_weight, 'grid', axis=0, tiled=True)  37.5 us
    all_gather x1, waiting for transfers between devices, shards(): lax.all_gather(key_weight, 'grid', axis=0, tiled=True)  37.2 us
    all_gather x1, blocking collectives, shards(): complete_head = lax.all_gather(head_weight, 'grid', axis=0, tiled=True)  25.1 us
    psum x1, waiting for transfers between devices, shards(): lax.psum(mixing_share.astype(jnp.bfloat16), 'member').astype(jnp.float32)  20.4 us
    all_gather x1, waiting for transfers between devices, shards(): full_out = lax.all_gather(output_weight, 'grid', axis=0, tiled=True)  19.6 us
    all_gather x1, waiting for transfers between devices, shards(): lax.all_gather(query_weight, 'grid', axis=0, tiled=True)  12.6 us
    scatter-add x1, other arithmetic, shards(): jax.ops.segment_sum(returned.reshape(points * KNB, 2 * inner_width), loca...  10.6 us
  transfers between devices with their start and end apart: 11, of which 9 were waited for; matrix products, arithmetic and copies ran while one was open for 19% of the time, Pallas kernels for 0%

commit v1 on v0

v1 whole, which is shorter than its diff:
```python
import functools
import math

import jax
import jax.numpy as jnp
from jax import lax
from jax.experimental import pallas as pl
from jax.experimental.pallas import tpu as pltpu
from jax.sharding import PartitionSpec as P

HEADS = 8
HALO = 32
MESH = pl.DeviceIdType.MESH

epsilon = 1e-05
smooth = 0.1

BF = jnp.bfloat16
F32 = jnp.float32


def dot(left, right, left_dim=1, right_dim=0):
    return lax.dot_general(
        left,
        right,
        (((left_dim,), (right_dim,)), ((), ())),
        preferred_element_type=F32,
    )


def gradient_of(spread):
    return spread * lax.rsqrt(spread * spread + smooth * smooth)


def factors(total):
    pair = 2 if total % 2 == 0 else 1
    near = 2 if (total // pair) % 2 == 0 else 1
    return total // (pair * near), near, pair


def kernel(
    members,
    grid,
    states,
    gain,
    wq,
    wk,
    wv,
    wo,
    wh,
    nb,
    obs,
    grad_input,
    grad_mixing,
    grad_head,
    grad_kv,
    qkv_all,
    wo_all,
    wh_all,
    centred,
    normed,
    query,
    ext,
    att,
    prob,
    mixed,
    layer_out,
    forecasts,
    grad_out,
    grad_mixed,
    grad_query,
    grad_ext,
    halo_out,
    halo_in,
    stage,
    shares,
    gather_send,
    gather_recv,
    halo_send,
    halo_recv,
    fore_send,
    fore_recv,
    share_send,
    share_recv,
):
    everyone = members * grid
    m = lax.axis_index("member")
    g = lax.axis_index("grid")
    me = m * grid + g
    points, width = states.shape[1], states.shape[2]
    inner = wq.shape[1]
    extent = points + 2 * HALO
    variables = obs.shape[1]
    head_dim = inner // HEADS
    far, near, pair = factors(grid)
    a, b, c = g // (near * pair), (g // pair) % near, g % pair

    def remote(src, dst, send, recv, mt, gt):
        return pltpu.make_async_remote_copy(
            src_ref=src,
            dst_ref=dst,
            send_sem=send,
            recv_sem=recv,
            device_id={"member": mt, "grid": gt},
            device_id_type=MESH,
        )

    barrier = pltpu.get_barrier_semaphore()

    def greet(i, carry):
        t = lax.rem(me + i, everyone)
        pl.semaphore_signal(
            barrier,
            inc=1,
            device_id={"member": t // grid, "grid": lax.rem(t, grid)},
            device_id_type=MESH,
        )
        return carry

    lax.fori_loop(1, everyone, greet, 0)

    qkv_all[g, :, 0:inner] = wq[...]
    qkv_all[g, :, inner : 2 * inner] = wk[...]
    qkv_all[g, :, 2 * inner : 3 * inner] = wv[...]
    wo_all[g] = wo[...]
    wh_all[g] = wh[...]
    pl.semaphore_wait(barrier, everyone - 1)

    pending = []

    def at(ai, bi, ci):
        return (ai * near + bi) * pair + ci

    def gather(buffers, base):
        counter = [0]

        def send(slot, gt):
            for n, buf in enumerate(buffers):
                copy = remote(
                    buf.at[slot],
                    buf.at[slot],
                    gather_send.at[base + n, counter[0]],
                    gather_recv.at[base + n, slot],
                    m,
                    gt,
                )
                copy.start()
                pending.append(copy)
            counter[0] += 1

        def arrived(slot):
            for n, buf in enumerate(buffers):
                remote(
                    buf.at[slot],
                    buf.at[slot],
                    gather_send.at[base + n, 0],
                    gather_recv.at[base + n, slot],
                    m,
                    g,
                ).wait_recv()

        other_b = lax.rem(b + 1, near)
        other_c = lax.rem(c + 1, pair)

        def begin():
            for i in range(1, far):
                send(g, at(lax.rem(a + i, far), b, c))
            if near > 1:
                send(g, at(a, other_b, c))
            if pair > 1:
                send(g, at(a, b, other_c))

        def from_far(i):
            slot = at(lax.rem(a + i, far), b, c)
            arrived(slot)
            if near > 1:
                send(slot, at(a, other_b, c))
            if pair > 1:
                send(slot, at(a, b, other_c))

        def from_near(i):
            slot = at(lax.rem(a + i, far), other_b, c)
            arrived(slot)
            if pair > 1:
                send(slot, at(a, b, other_c))

        steps = []
        for i in range(1, far):
            steps.append(functools.partial(from_far, i))
            if near > 1:
                steps.append(functools.partial(from_near, i - 1))
        if near > 1:
            steps.append(functools.partial(from_near, far - 1))

        def finish():
            if pair > 1:
                for i in range(far):
                    for j in range(near):
                        arrived(at(lax.rem(a + i, far), lax.rem(b + j, near), other_c))

        return begin, steps, finish

    begin_qkv, steps_qkv, finish_qkv = gather([qkv_all], 0)
    begin_out, steps_out, finish_out = gather([wo_all, wh_all], 1)

    begin_qkv()

    x = states[0].astype(F32)
    center = x - jnp.mean(x, axis=-1, keepdims=True)
    inverse = lax.rsqrt(jnp.mean(center * center, axis=-1, keepdims=True) + epsilon)
    centred[...] = center * inverse
    normed[...] = (centred[...] * gain[...]).astype(BF)

    local = nb[...] - (g * points - HALO)
    column = lax.broadcasted_iota(jnp.int32, (points, extent), 1)
    count = jnp.zeros((points, extent), F32)
    for k in range(nb.shape[1]):
        count = count + (local[:, k : k + 1] == column).astype(F32)
    count2 = jnp.concatenate([count, count], axis=0)

    for step in steps_qkv:
        step()
    begin_out()
    finish_qkv()

    kv = dot(normed[...], qkv_all[:, :, inner : 3 * inner].reshape(width, 2 * inner))
    ext[HALO : HALO + points, :] = kv.astype(BF)
    after, before = lax.rem(g + 1, grid), lax.rem(g + grid - 1, grid)
    up = remote(
        ext.at[pl.ds(points, HALO)],
        ext.at[pl.ds(0, HALO)],
        halo_send.at[0],
        halo_recv.at[0],
        m,
        after,
    )
    down = remote(
        ext.at[pl.ds(HALO, HALO)],
        ext.at[pl.ds(points + HALO, HALO)],
        halo_send.at[1],
        halo_recv.at[1],
        m,
        before,
    )
    up.start()
    down.start()
    query[...] = dot(
        normed[...], qkv_all[:, :, 0:inner].reshape(width, inner)
    ).astype(BF)
    up.wait()
    down.wait()

    lanes = 2 * head_dim
    first = lax.broadcasted_iota(jnp.int32, (points, lanes), 1) < head_dim
    scale = 1.0 / math.sqrt(head_dim)

    def stacked(rows):
        zero = jnp.zeros_like(rows)
        return jnp.concatenate(
            [jnp.where(first, rows, zero), jnp.where(first, zero, rows)], axis=0
        )

    def merged(rows):
        return jnp.where(first, rows[:points], rows[points:])

    couples = HEADS // 2
    per = -(-len(steps_out) // couples)
    for p in range(couples):
        cols = slice(p * lanes, (p + 1) * lanes)
        vcols = slice(inner + p * lanes, inner + (p + 1) * lanes)
        q2 = stacked(query[:, cols])
        score = dot(q2, ext[:, cols], 1, 1) * scale
        score = jnp.where(count2 > 0, score, -1e30)
        highest = jnp.max(score, axis=-1, keepdims=True)
        e = jnp.exp(score - highest)
        attention = e / jnp.sum(e * count2, axis=-1, keepdims=True)
        att[p] = attention
        weight = (attention.astype(BF).astype(F32) * count2).astype(BF)
        prob[p] = weight
        mixed[:, cols] = merged(dot(weight, ext[:, vcols])).astype(BF)
        for step in steps_out[p * per : (p + 1) * per]:
            step()
    finish_out()

    out_full = wo_all[...].reshape(inner, width)
    head_full = wh_all[...].reshape(width, variables)
    layer_out[...] = (states[0].astype(F32) + dot(mixed[...], out_full)).astype(BF)
    forecasts[m] = dot(layer_out[...], head_full)
    fore = []
    for i in range(1, members):
        copy = remote(
            forecasts.at[m],
            forecasts.at[m],
            fore_send.at[i],
            fore_recv.at[m],
            lax.rem(m + i, members),
            g,
        )
        copy.start()
        fore.append(copy)
    mine = forecasts[m]
    slope = gradient_of(mine - obs[...])
    for i in range(1, members):
        j = lax.rem(m + i, members)
        remote(
            forecasts.at[j], forecasts.at[j], fore_send.at[i], fore_recv.at[j], m, g
        ).wait_recv()
        slope = slope - gradient_of(mine - forecasts[j]) / (members - 1)
    grad_fore = slope.astype(BF)

    rows_head, rows_mix = wh.shape[0], wo.shape[0]
    stage[:, 0:rows_head, :] = (
        dot(layer_out[...], grad_fore, 0, 0)
        .astype(BF)
        .reshape(grid, rows_head, variables)
    )
    stage[:, rows_head : rows_head + rows_mix, :] = (
        dot(mixed[...], grad_fore, 0, 0).astype(BF).reshape(grid, rows_mix, variables)
    )

    def share(i):
        t = lax.rem(me + i, everyone)
        gt = lax.rem(t, grid)
        return remote(
            stage.at[gt],
            shares.at[me],
            share_send.at[i],
            share_recv.at[me],
            t // grid,
            gt,
        )

    def share_start(i, carry):
        share(i).start()
        return carry

    lax.fori_loop(1, everyone, share_start, 0)

    grad_out[...] = dot(grad_fore, head_full, 1, 1)
    grad_mixed[...] = dot(grad_out[...].astype(BF), out_full, 1, 1).astype(BF)

    for p in range(couples):
        cols = slice(p * lanes, (p + 1) * lanes)
        vcols = slice(inner + p * lanes, inner + (p + 1) * lanes)
        q2 = stacked(query[:, cols])
        g2 = stacked(grad_mixed[:, cols])
        attention = att[p]
        grad_prob = dot(g2, ext[:, vcols], 1, 1)
        weighted = attention * count2
        middle = jnp.sum(weighted * grad_prob, axis=-1, keepdims=True)
        grad_score = (weighted * (grad_prob - middle) * scale).astype(BF)
        grad_ext[:, cols] = dot(grad_score, q2, 0, 0)
        grad_ext[:, vcols] = dot(prob[p], g2, 0, 0)
        grad_query[:, cols] = merged(dot(grad_score, ext[:, cols])).astype(BF)

    halo_out[0] = grad_ext[0:HALO, :].astype(BF)
    halo_out[1] = grad_ext[points + HALO : points + 2 * HALO, :].astype(BF)
    back_down = remote(
        halo_out.at[0], halo_in.at[0], halo_send.at[2], halo_recv.at[2], m, before
    )
    back_up = remote(
        halo_out.at[1], halo_in.at[1], halo_send.at[3], halo_recv.at[3], m, after
    )
    back_down.start()
    back_up.start()
    grad_normed = dot(
        grad_query[...], qkv_all[:, :, 0:inner].reshape(width, inner), 1, 1
    )
    back_down.wait()
    back_up.wait()
    grad_kv[0] = grad_ext[HALO : HALO + points, :]
    grad_kv[0, 0:HALO, :] += halo_in[1].astype(F32)
    grad_kv[0, points - HALO : points, :] += halo_in[0].astype(F32)
    grad_normed = grad_normed + dot(
        grad_kv[0].astype(BF),
        qkv_all[:, :, inner : 3 * inner].reshape(width, 2 * inner),
        1,
        1,
    )
    gg = grad_normed * gain[...]
    cen = centred[...]
    grad_states = inverse * (
        gg
        - jnp.mean(gg, axis=-1, keepdims=True)
        - cen * jnp.mean(gg * cen, axis=-1, keepdims=True)
    )
    grad_input[0] = (grad_out[...] + grad_states).astype(BF)

    def share_sum(i, total):
        s = lax.rem(me + everyone - i, everyone)
        remote(
            stage.at[g], shares.at[s], share_send.at[i], share_recv.at[s], m, g
        ).wait_recv()
        return total + shares[s].astype(F32)

    total = lax.fori_loop(1, everyone, share_sum, stage[g].astype(F32))
    scaling = 1.0 / math.sqrt(members * grid * points)
    grad_head[...] = total[0:rows_head] * scaling
    grad_mixing[...] = (
        dot(total[rows_head : rows_head + rows_mix].astype(BF), head_full, 1, 1)
        * scaling
    )

    def share_done(i, carry):
        share(i).wait_send()
        return carry

    lax.fori_loop(1, everyone, share_done, 0)
    for copy in pending:
        copy.wait_send()
    for copy in fore:
        copy.wait_send()


def solution(mesh):
    members, grid = mesh.shape["member"], mesh.shape["grid"]
    far, near, pair = factors(grid)

    def shards(states, gain, wq, wk, wv, wo, wh, nb, obs):
        points, width = states.shape[1], states.shape[2]
        inner = wq.shape[1]
        variables = obs.shape[1]
        extent = points + 2 * HALO
        everyone = members * grid
        slab = wh.shape[0] + wo.shape[0]
        sends = grid
        vm = pltpu.VMEM
        dma = pltpu.SemaphoreType.DMA
        couples = HEADS // 2
        return pl.pallas_call(
            functools.partial(kernel, members, grid),
            out_shape=(
                jax.ShapeDtypeStruct((1, points, width), BF),
                jax.ShapeDtypeStruct(wo.shape, F32),
                jax.ShapeDtypeStruct(wh.shape, F32),
                jax.ShapeDtypeStruct((1, points, 2 * inner), F32),
            ),
            in_specs=[pl.BlockSpec(memory_space=pltpu.VMEM)] * 9,
            out_specs=(pl.BlockSpec(memory_space=pltpu.VMEM),) * 4,
            scratch_shapes=[
                vm((grid, wq.shape[0], 3 * inner), BF),
                vm((grid,) + wo.shape, BF),
                vm((grid,) + wh.shape, BF),
                vm((points, width), F32),
                vm((points, width), BF),
                vm((points, inner), BF),
                vm((extent, 2 * inner), BF),
                vm((couples, 2 * points, extent), F32),
                vm((couples, 2 * points, extent), BF),
                vm((points, inner), BF),
                vm((points, width), BF),
                vm((members, points, variables), F32),
                vm((points, width), F32),
                vm((points, inner), BF),
                vm((points, inner), BF),
                vm((extent, 2 * inner), F32),
                vm((2, HALO, 2 * inner), BF),
                vm((2, HALO, 2 * inner), BF),
                vm((grid, slab, variables), BF),
                vm((everyone, slab, variables), BF),
                dma((3, sends)),
                dma((3, grid)),
                dma((4,)),
                dma((4,)),
                dma((members,)),
                dma((members,)),
                dma((everyone,)),
                dma((everyone,)),
            ],
            compiler_params=pltpu.CompilerParams(
                collective_id=0,
                has_side_effects=True,
                vmem_limit_bytes=44 * 1024 * 1024,
            ),
        )(states, gain.reshape(1, width), wq, wk, wv, wo, wh, nb, obs)

    return jax.shard_map(
        shards,
        mesh=mesh,
        in_specs=(
            P("member", "grid", None),
            P(),
            P("grid", None),
            P("grid", None),
            P("grid", None),
            P("grid", None),
            P("grid", None),
            P("grid", None),
            P("grid", None),
        ),
        out_specs=(
            P("member", "grid", None),
            P("grid", None),
            P("grid", None),
            P("member", "grid", None),
        ),
        check_vma=False,
    )
```

time: 328 us -> 87.5 us (0.27)
  the two profiles are of different devices: /device:TPU:0 before, /device:TPU:16 now
where the time goes in v1:
time: 87.5 us; the launch traced here: 87 us
  Pallas kernels  77.7 us (89%)
  local copies, waits for them, and re-layouts  8.61 us (10%)
    pallas_call x1, Pallas kernels, shards(): pl.pallas_call(functools.partial(kernel, members, grid), out_shape=(jax.S...  77.7 us
    unnamed x21, local copies, waits for them, and re-layouts  8.61 us

profile of v1, /device:TPU:16, one launch (start us, length us, event | category | flops | bytes accessed | tf_op | source)
XLA Modules:
  0.0 87.0 jit_solution(12687016075169433800)
XLA Ops:
  0.6 0.0 copy-start.1
  0.6 0.0 copy-start.7
  0.7 0.8 copy.13.nb
  1.5 0.0 copy-done.1
  1.5 0.0 copy-done.7
  1.5 0.0 copy-start
  1.5 0.9 %copy-done = bf16[1,128,1024]{2,1,0:T(8,128)(2,1)S(1)} copy-done((bf16[1,128,1024]{2,1,0:T(8,128)(2,1)S(1)}, bf16[1,128,1024]{2,1,0:T(8,128)(2,1)}, u32[]{:S(2)}) %copy-start) | copy-done | bytes 262168
  2.4 0.0 copy-start.2
  2.4 0.8 copy-done.2
  3.3 0.0 copy-start.3
  3.3 0.8 copy-done.3
  4.1 0.0 copy-start.4
  4.1 0.8 copy-done.4
  5.0 0.0 copy-start.5
  5.0 0.8 copy-done.5
  5.8 0.0 copy-start.6
  5.8 0.7 copy-done.6
  6.5 77.7 %shard_map.120 = (bf16[1,128,1024]{2,1,0:T(8,128)(2,1)S(1)}, f32[32,1024]{1,0:T(8,128)S(1)}, f32[64,128]{1,0:T(8,128)S(1)}, f32[1,128,1024]{2,1,0:T(8,128)S(1)}) custom-call(bf16[1,128,1024]{2,1,0:T(8,128)(2,1)S(1)} %copy-done, f32[1,1024]{1,0:T(1,128)S(1)} %bitcast.1, bf16[64,512]{1,0:T(8,128)(2,1)S(1)} %copy-done.1, bf16[64,512]{1,0:T(8,128)(2,1)S(1)} %copy-done.2, ...), custom_call_target="tpu_custom_call" | custom-call | tf_op jit(solution)/shard_map/pallas_call | solution.py:430
  84.3 0.7 copy.18
  85.0 0.7 copy.19
  85.6 0.6 copy.20
  86.2 0.8 copy.21
Async XLA Ops:
  0.6 0.8 copy-start.1
  0.6 0.8 copy-start.7
  1.5 1.0 %copy-start = (bf16[1,128,1024]{2,1,0:T(8,128)(2,1)S(1)}, bf16[1,128,1024]{2,1,0:T(8,128)(2,1)}, u32[]{:S(2)}) copy-start(bf16[1,128,1024]{2,1,0:T(8,128)(2,1)} %states.1) | copy-start | bytes 786436
  2.4 0.8 copy-start.2
  3.3 0.8 copy-start.3
  4.1 0.8 copy-start.4
  5.0 0.8 copy-start.5
  5.8 0.7 copy-start.6

commit v2 on v1

--- a/solution.py
+++ b/solution.py
@@ -41,19 +41,23 @@
 def kernel(
     members,
     grid,
-    states,
-    gain,
+    states_hbm,
+    gain_hbm,
     wq,
     wk,
     wv,
     wo,
     wh,
-    nb,
-    obs,
+    nb_hbm,
+    obs_hbm,
     grad_input,
     grad_mixing,
     grad_head,
     grad_kv,
+    states,
+    gain,
+    nb,
+    obs,
     qkv_all,
     wo_all,
     wh_all,
@@ -73,7 +77,11 @@
     halo_out,
     halo_in,
     stage,
+    sibling,
+    stage_sum,
     shares,
+    totals,
+    load_sem,
     gather_send,
     gather_recv,
     halo_send,
@@ -82,11 +90,11 @@
     fore_recv,
     share_send,
     share_recv,
+    total_send,
+    total_recv,
 ):
-    everyone = members * grid
     m = lax.axis_index("member")
     g = lax.axis_index("grid")
-    me = m * grid + g
     points, width = states.shape[1], states.shape[2]
     inner = wq.shape[1]
     extent = points + 2 * HALO
@@ -94,6 +102,8 @@
     head_dim = inner // HEADS
     far, near, pair = factors(grid)
     a, b, c = g // (near * pair), (g // pair) % near, g % pair
+    quads, quad = grid // pair, g // pair
+    after, before = lax.rem(g + 1, grid), lax.rem(g + grid - 1, grid)
 
     def remote(src, dst, send, recv, mt, gt):
         return pltpu.make_async_remote_copy(
@@ -105,84 +115,174 @@
             device_id_type=MESH,
         )
 
+    loads = [
+        pltpu.make_async_copy(src, dst, load_sem.at[n])
+        for n, (src, dst) in enumerate(
+            [
+                (wq, qkv_all.at[g, :, pl.ds(0, inner)]),
+                (wk, qkv_all.at[g, :, pl.ds(inner, inner)]),
+                (wv, qkv_all.at[g, :, pl.ds(2 * inner, inner)]),
+                (states_hbm, states),
+                (gain_hbm, gain),
+                (nb_hbm, nb),
+                (wo, wo_all.at[g]),
+                (wh, wh_all.at[g]),
+                (obs_hbm, obs),
+            ]
+        )
+    ]
+    for load in loads:
+        load.start()
+
     barrier = pltpu.get_barrier_semaphore()
-
-    def greet(i, carry):
-        t = lax.rem(me + i, everyone)
+    peers = [(m, after), (m, before)]
+    peers += [(m, lax.rem(quad + i, quads) * pair + c) for i in range(1, quads)]
+    peers += [(m, quad * pair + lax.rem(c + i, pair)) for i in range(1, pair)]
+    peers += [(lax.rem(m + i, members), g) for i in range(1, members)]
+    for mt, gt in peers:
         pl.semaphore_signal(
-            barrier,
-            inc=1,
-            device_id={"member": t // grid, "grid": lax.rem(t, grid)},
-            device_id_type=MESH,
+            barrier, inc=1, device_id={"member": mt, "grid": gt}, device_id_type=MESH
         )
-        return carry
-
-    lax.fori_loop(1, everyone, greet, 0)
-
-    qkv_all[g, :, 0:inner] = wq[...]
-    qkv_all[g, :, inner : 2 * inner] = wk[...]
-    qkv_all[g, :, 2 * inner : 3 * inner] = wv[...]
-    wo_all[g] = wo[...]
-    wh_all[g] = wh[...]
-    pl.semaphore_wait(barrier, everyone - 1)
+    for load in loads[:3]:
+        load.wait()
+    pl.semaphore_wait(barrier, len(peers))
 
     pending = []
 
     def at(ai, bi, ci):
         return (ai * near + bi) * pair + ci
 
-    def gather(buffers, base):
+    def along(i):
+        if i == 0:
+            return a
+        if far != 4:
+            return lax.rem(a + i, far)
+        if i == 1:
+            return a + 1 - 2 * lax.rem(a, 2)
+        if i == 2:
+            return lax.rem(a + 2, 4)
+        return 3 - a
+
+    other_m, other_b, other_c = 1 - m, lax.rem(b + 1, near), lax.rem(c + 1, pair)
+    line = [2, 1, 3] if far == 4 else list(range(1, far))
+
+    def gather(buf, base, split):
         counter = [0]
-
-        def send(slot, gt):
-            for n, buf in enumerate(buffers):
-                copy = remote(
-                    buf.at[slot],
-                    buf.at[slot],
-                    gather_send.at[base + n, counter[0]],
-                    gather_recv.at[base + n, slot],
-                    m,
-                    gt,
-                )
-                copy.start()
-                pending.append(copy)
+        quarter = buf.shape[2] // 4
+
+        def piece(slot, kind):
+            name, n = kind
+            if name == "full":
+                return buf.at[slot], gather_recv.at[base, 6, slot]
+            if name == "half":
+                start = pl.multiple_of(2 * quarter * n, 128)
+                view = buf.at[slot, :, pl.ds(start, 2 * quarter)]
+                return view, gather_recv.at[base, n, slot]
+            view = buf.at[slot, :, pl.ds(pl.multiple_of(quarter * n, 128), quarter)]
+            return view, gather_recv.at[base, 2 + n, slot]
+
+        def send(slot, kind, mt, gt):
+            view, recv = piece(slot, kind)
+            copy = remote(view, view, gather_send.at[base, counter[0]], recv, mt, gt)
+            copy.start()
+            pending.append(copy)
             counter[0] += 1
 
-        def arrived(slot):
-            for n, buf in enumerate(buffers):
-                remote(
-                    buf.at[slot],
-                    buf.at[slot],
-                    gather_send.at[base + n, 0],
-                    gather_recv.at[base + n, slot],
-                    m,
-                    g,
-                ).wait_recv()
-
-        other_b = lax.rem(b + 1, near)
-        other_c = lax.rem(c + 1, pair)
+        def arrived(slot, kind):
+            view, recv = piece(slot, kind)
+            remote(view, view, gather_send.at[base, 0], recv, m, g).wait_recv()
+
+        full = ("full", 0)
+        y_peer, core_peer, x_peer = at(a, other_b, c), at(a, b, other_c), g
+
+        if split:
+            mine, theirs = ("half", m), ("half", other_m)
+            extra, rest_in = ("quarter", 2 * other_m), ("quarter", 2 * other_m + 1)
+            rest_out = ("quarter", 2 * m + 1)
+
+            def begin():
+                for i in line:
+                    send(g, mine, m, at(along(i), b, c))
+                send(g, mine, m, y_peer)
+                send(g, extra, m, y_peer)
+                send(g, full, m, core_peer)
+
+            def from_line(i):
+                slot = at(along(i), b, c)
+                arrived(slot, mine)
+                send(slot, mine, other_m, x_peer)
+                send(slot, mine, m, y_peer)
+                send(slot, mine, m, core_peer)
+
+            def from_x(i):
+                slot = at(along(i), b, c)
+                arrived(slot, theirs)
+                send(slot, extra, m, y_peer)
+                send(slot, theirs, m, core_peer)
+
+            def from_y(i):
+                slot = at(along(i), other_b, c)
+                arrived(slot, mine)
+                send(slot, rest_out, other_m, x_peer)
+                send(slot, mine, m, core_peer)
+
+            def from_y_extra(i):
+                slot = at(along(i), other_b, c)
+                arrived(slot, extra)
+                send(slot, extra, m, core_peer)
+
+            def from_x_rest(i):
+                slot = at(along(i), other_b, c)
+                arrived(slot, rest_in)
+                send(slot, rest_in, m, core_peer)
+
+            part = functools.partial
+            steps = []
+            for i in range(far):
+                if i + 1 < far:
+                    steps.append(part(from_line, i + 1))
+                steps.append(part(from_y, i))
+                if i + 1 < far:
+                    steps.append(part(from_x, i + 1))
+                steps.append(part(from_y_extra, i))
+                steps.append(part(from_x_rest, i))
+
+            def finish():
+                for i in range(far):
+                    slot = at(along(i), b, other_c)
+                    if i == 0:
+                        arrived(slot, full)
+                    else:
+                        arrived(slot, mine)
+                        arrived(slot, theirs)
+                    slot = at(along(i), other_b, other_c)
+                    arrived(slot, mine)
+                    arrived(slot, extra)
+                    arrived(slot, rest_in)
+
+            return begin, steps, finish
 
         def begin():
-            for i in range(1, far):
-                send(g, at(lax.rem(a + i, far), b, c))
+            for i in line:
+                send(g, full, m, at(along(i), b, c))
             if near > 1:
-                send(g, at(a, other_b, c))
+                send(g, full, m, y_peer)
             if pair > 1:
-                send(g, at(a, b, other_c))
+                send(g, full, m, core_peer)
 
         def from_far(i):
-            slot = at(lax.rem(a + i, far), b, c)
-            arrived(slot)
+            slot = at(along(i), b, c)
+            arrived(slot, full)
             if near > 1:
-                send(slot, at(a, other_b, c))
+                send(slot, full, m, y_peer)
             if pair > 1:
-                send(slot, at(a, b, other_c))
+                send(slot, full, m, core_peer)
 
         def from_near(i):
-            slot = at(lax.rem(a + i, far), other_b, c)
-            arrived(slot)
+            slot = at(along(i), other_b, c)
+            arrived(slot, full)
             if pair > 1:
-                send(slot, at(a, b, other_c))
+                send(slot, full, m, core_peer)
 
         steps = []
         for i in range(1, far):
@@ -195,37 +295,48 @@
         def finish():
             if pair > 1:
                 for i in range(far):
-                    for j in range(near):
-                        arrived(at(lax.rem(a + i, far), lax.rem(b + j, near), other_c))
+                    arrived(at(along(i), b, other_c), full)
+                    if near > 1:
+                        arrived(at(along(i), other_b, other_c), full)
 
         return begin, steps, finish
 
-    begin_qkv, steps_qkv, finish_qkv = gather([qkv_all], 0)
-    begin_out, steps_out, finish_out = gather([wo_all, wh_all], 1)
+    split = members == 2 and near == 2 and pair == 2
+    begin_qkv, steps_qkv, finish_qkv = gather(qkv_all, 0, split)
+    begin_wo, steps_wo, finish_wo = gather(wo_all, 1, split)
+    begin_wh, steps_wh, finish_wh = gather(wh_all, 2, False)
 
     begin_qkv()
 
+    for load in loads[3:]:
+        load.wait()
     x = states[0].astype(F32)
     center = x - jnp.mean(x, axis=-1, keepdims=True)
     inverse = lax.rsqrt(jnp.mean(center * center, axis=-1, keepdims=True) + epsilon)
     centred[...] = center * inverse
     normed[...] = (centred[...] * gain[...]).astype(BF)
 
-    local = nb[...] - (g * points - HALO)
+    local = nb[...].T - (g * points - HALO)
     column = lax.broadcasted_iota(jnp.int32, (points, extent), 1)
     count = jnp.zeros((points, extent), F32)
-    for k in range(nb.shape[1]):
+    for k in range(nb.shape[0]):
         count = count + (local[:, k : k + 1] == column).astype(F32)
     count2 = jnp.concatenate([count, count], axis=0)
 
     for step in steps_qkv:
         step()
-    begin_out()
+    begin_wo()
+    begin_wh()
     finish_qkv()
+    steps_out = []
+    for n, step in enumerate(steps_wo):
+        steps_out.append(step)
+        if n % 2 == 1:
+            steps_out += steps_wh[n // 2 : n // 2 + 1]
+    steps_out += steps_wh[len(steps_wo) // 2 :]
 
     kv = dot(normed[...], qkv_all[:, :, inner : 3 * inner].reshape(width, 2 * inner))
     ext[HALO : HALO + points, :] = kv.astype(BF)
-    after, before = lax.rem(g + 1, grid), lax.rem(g + grid - 1, grid)
     up = remote(
         ext.at[pl.ds(points, HALO)],
         ext.at[pl.ds(0, HALO)],
@@ -280,7 +391,8 @@
         mixed[:, cols] = merged(dot(weight, ext[:, vcols])).astype(BF)
         for step in steps_out[p * per : (p + 1) * per]:
             step()
-    finish_out()
+    finish_wo()
+    finish_wh()
 
     out_full = wo_all[...].reshape(inner, width)
     head_full = wh_all[...].reshape(width, variables)
@@ -309,35 +421,51 @@
     grad_fore = slope.astype(BF)
 
     rows_head, rows_mix = wh.shape[0], wo.shape[0]
-    stage[:, 0:rows_head, :] = (
+    head_part = (
         dot(layer_out[...], grad_fore, 0, 0)
         .astype(BF)
-        .reshape(grid, rows_head, variables)
-    )
-    stage[:, rows_head : rows_head + rows_mix, :] = (
-        dot(mixed[...], grad_fore, 0, 0).astype(BF).reshape(grid, rows_mix, variables)
-    )
-
-    def share(i):
-        t = lax.rem(me + i, everyone)
-        gt = lax.rem(t, grid)
-        return remote(
-            stage.at[gt],
-            shares.at[me],
-            share_send.at[i],
-            share_recv.at[me],
-            t // grid,
-            gt,
-        )
-
-    def share_start(i, carry):
-        share(i).start()
-        return carry
-
-    lax.fori_loop(1, everyone, share_start, 0)
+        .reshape(quads, pair, rows_head, variables)
+    )
+    mix_part = (
+        dot(mixed[...], grad_fore, 0, 0)
+        .astype(BF)
+        .reshape(quads, pair, rows_mix, variables)
+    )
+    for n in range(pair):
+        stage[n, :, 0:rows_head, :] = head_part[:, n]
+        stage[n, :, rows_head : rows_head + rows_mix, :] = mix_part[:, n]
+    crossing = remote(
+        stage.at[other_c],
+        sibling,
+        share_send.at[0],
+        share_recv.at[quads],
+        m,
+        at(a, b, other_c),
+    )
+    if pair > 1:
+        crossing.start()
 
     grad_out[...] = dot(grad_fore, head_full, 1, 1)
     grad_mixed[...] = dot(grad_out[...].astype(BF), out_full, 1, 1).astype(BF)
+
+    if pair > 1:
+        crossing.wait()
+        stage_sum[...] = (stage[c].astype(F32) + sibling[...].astype(F32)).astype(BF)
+    else:
+        stage_sum[...] = stage[0]
+    sharing = []
+    for i in range(1, quads):
+        t = lax.rem(quad + i, quads)
+        copy = remote(
+            stage_sum.at[t],
+            shares.at[quad],
+            share_send.at[i],
+            share_recv.at[quad],
+            m,
+            t * pair + c,
+        )
+        copy.start()
+        sharing.append(copy)
 
     for p in range(couples):
         cols = slice(p * lanes, (p + 1) * lanes)
@@ -377,6 +505,25 @@
         1,
         1,
     )
+    total = stage_sum[quad].astype(F32)
+    for i in range(1, quads):
+        t = lax.rem(quad + quads - i, quads)
+        remote(
+            stage_sum.at[t], shares.at[t], share_send.at[i], share_recv.at[t], m, g
+        ).wait_recv()
+        total = total + shares[t].astype(F32)
+    totals[m] = total.astype(BF)
+    for i in range(1, members):
+        copy = remote(
+            totals.at[m],
+            totals.at[m],
+            total_send.at[i],
+            total_recv.at[m],
+            lax.rem(m + i, members),
+            g,
+        )
+        copy.start()
+        sharing.append(copy)
     gg = grad_normed * gain[...]
     cen = centred[...]
     grad_states = inverse * (
@@ -386,14 +533,13 @@
     )
     grad_input[0] = (grad_out[...] + grad_states).astype(BF)
 
-    def share_sum(i, total):
-        s = lax.rem(me + everyone - i, everyone)
+    total = totals[m].astype(F32)
+    for i in range(1, members):
+        j = lax.rem(m + i, members)
         remote(
-            stage.at[g], shares.at[s], share_send.at[i], share_recv.at[s], m, g
+            totals.at[j], totals.at[j], total_send.at[i], total_recv.at[j], m, g
         ).wait_recv()
-        return total + shares[s].astype(F32)
-
-    total = lax.fori_loop(1, everyone, share_sum, stage[g].astype(F32))
+        total = total + totals[j].astype(F32)
     scaling = 1.0 / math.sqrt(members * grid * points)
     grad_head[...] = total[0:rows_head] * scaling
     grad_mixing[...] = (
@@ -401,14 +547,7 @@
         * scaling
     )
 
-    def share_done(i, carry):
-        share(i).wait_send()
-        return carry
-
-    lax.fori_loop(1, everyone, share_done, 0)
-    for copy in pending:
-        copy.wait_send()
-    for copy in fore:
+    for copy in pending + fore + sharing:
         copy.wait_send()
 
 
@@ -421,9 +560,9 @@
         inner = wq.shape[1]
         variables = obs.shape[1]
         extent = points + 2 * HALO
-        everyone = members * grid
+        quads = grid // pair
         slab = wh.shape[0] + wo.shape[0]
-        sends = grid
+        sends = 4 * grid
         vm = pltpu.VMEM
         dma = pltpu.SemaphoreType.DMA
         couples = HEADS // 2
@@ -435,9 +574,13 @@
                 jax.ShapeDtypeStruct(wh.shape, F32),
                 jax.ShapeDtypeStruct((1, points, 2 * inner), F32),
             ),
-            in_specs=[pl.BlockSpec(memory_space=pltpu.VMEM)] * 9,
+            in_specs=[pl.BlockSpec(memory_space=pl.ANY)] * 9,
             out_specs=(pl.BlockSpec(memory_space=pltpu.VMEM),) * 4,
             scratch_shapes=[
+                vm(states.shape, BF),
+                vm((1, width), F32),
+                vm((nb.shape[1], nb.shape[0]), jnp.int32),
+                vm(obs.shape, F32),
                 vm((grid, wq.shape[0], 3 * inner), BF),
                 vm((grid,) + wo.shape, BF),
                 vm((grid,) + wh.shape, BF),
@@ -456,23 +599,29 @@
                 vm((extent, 2 * inner), F32),
                 vm((2, HALO, 2 * inner), BF),
                 vm((2, HALO, 2 * inner), BF),
-                vm((grid, slab, variables), BF),
-                vm((everyone, slab, variables), BF),
+                vm((pair, quads, slab, variables), BF),
+                vm((quads, slab, variables), BF),
+                vm((quads, slab, variables), BF),
+                vm((quads, slab, variables), BF),
+                vm((members, slab, variables), BF),
+                dma((9,)),
                 dma((3, sends)),
-                dma((3, grid)),
+                dma((3, 7, grid)),
                 dma((4,)),
                 dma((4,)),
                 dma((members,)),
                 dma((members,)),
-                dma((everyone,)),
-                dma((everyone,)),
+                dma((quads,)),
+                dma((quads + 1,)),
+                dma((members,)),
+                dma((members,)),
             ],
             compiler_params=pltpu.CompilerParams(
                 collective_id=0,
                 has_side_effects=True,
                 vmem_limit_bytes=44 * 1024 * 1024,
             ),
-        )(states, gain.reshape(1, width), wq, wk, wv, wo, wh, nb, obs)
+        )(states, gain.reshape(1, width), wq, wk, wv, wo, wh, nb.T, obs)
 
     return jax.shard_map(
         shards,

time: 87.5 us -> 82.1 us (0.938)
  the two profiles are of different devices: /device:TPU:16 before, /device:TPU:0 now
where the time goes in v2:
time: 82.1 us; the launch traced here: 81.7 us
  Pallas kernels  71 us (86%)
  local copies, waits for them, and re-layouts  9.99 us (12%)
    pallas_call x1, Pallas kernels, shards(): pl.pallas_call(functools.partial(kernel, members, grid), out_shape=(jax.S...  71 us
    unnamed x22, local copies, waits for them, and re-layouts  9.99 us

profile of v2, /device:TPU:0, one launch (start us, length us, event | category | flops | bytes accessed | tf_op | source)
XLA Modules:
  0.0 81.7 jit_solution(15949080141021916617)
XLA Ops:
  0.6 0.0 copy-start
  0.6 0.9 %copy-done = bf16[1,128,1024]{2,1,0:T(8,128)(2,1)S(1)} copy-done((bf16[1,128,1024]{2,1,0:T(8,128)(2,1)S(1)}, bf16[1,128,1024]{2,1,0:T(8,128)(2,1)}, u32[]{:S(2)}) %copy-start) | copy-done | bytes 262168
  1.6 0.0 copy-start.1
  1.6 0.8 %copy-done.1 = bf16[64,512]{1,0:T(8,128)(2,1)S(1)} copy-done((bf16[64,512]{1,0:T(8,128)(2,1)S(1)}, bf16[64,512]{1,0:T(8,128)(2,1)}, u32[]{:S(2)}) %copy-start.1) | copy-done | bytes 65560
  2.4 0.0 copy-start.2
  2.4 0.8 %copy-done.2 = bf16[64,512]{1,0:T(8,128)(2,1)S(1)} copy-done((bf16[64,512]{1,0:T(8,128)(2,1)S(1)}, bf16[64,512]{1,0:T(8,128)(2,1)}, u32[]{:S(2)}) %copy-start.2) | copy-done | bytes 65560
  3.3 0.0 copy-start.3
  3.3 0.8 %copy-done.3 = bf16[64,512]{1,0:T(8,128)(2,1)S(1)} copy-done((bf16[64,512]{1,0:T(8,128)(2,1)S(1)}, bf16[64,512]{1,0:T(8,128)(2,1)}, u32[]{:S(2)}) %copy-start.3) | copy-done | bytes 65560
  4.1 0.0 copy-start.4
  4.1 0.8 %copy-done.4 = bf16[32,1024]{1,0:T(8,128)(2,1)S(1)} copy-done((bf16[32,1024]{1,0:T(8,128)(2,1)S(1)}, bf16[32,1024]{1,0:T(8,128)(2,1)}, u32[]{:S(2)}) %copy-start.4) | copy-done | bytes 65560
  4.9 0.0 copy-start.5
  4.9 0.8 %copy-done.5 = f32[128,128]{1,0:T(8,128)S(1)} copy-done((f32[128,128]{1,0:T(8,128)S(1)}, f32[128,128]{1,0:T(8,128)}, u32[]{:S(2)}) %copy-start.5) | copy-done | bytes 65560
  5.8 0.0 copy-start.6
  5.8 0.7 copy-done.6
  6.5 0.0 copy-start.7
  6.5 0.7 copy-done.7
  7.2 0.0 copy-start.8
  7.2 0.7 copy-done.8
  7.9 71.0 %shard_map.120 = (bf16[1,128,1024]{2,1,0:T(8,128)(2,1)S(1)}, f32[32,1024]{1,0:T(8,128)S(1)}, f32[64,128]{1,0:T(8,128)S(1)}, f32[1,128,1024]{2,1,0:T(8,128)S(1)}) custom-call(bf16[1,128,1024]{2,1,0:T(8,128)(2,1)S(1)} %copy-done, f32[1,1024]{1,0:T(1,128)S(1)} %bitcast.2, bf16[64,512]{1,0:T(8,128)(2,1)S(1)} %copy-done.1, bf16[64,512]{1,0:T(8,128)(2,1)S(1)} %copy-done.2, ...), custom_call_target="tpu_custom_call" | custom-call | tf_op jit(solution)/shard_map/pallas_call | solution.py:569
  78.9 0.7 copy.17
  79.6 0.7 copy.18
  80.2 0.6 copy.19
  80.9 0.8 copy.20
Async XLA Ops:
  0.6 1.0 %copy-start = (bf16[1,128,1024]{2,1,0:T(8,128)(2,1)S(1)}, bf16[1,128,1024]{2,1,0:T(8,128)(2,1)}, u32[]{:S(2)}) copy-start(bf16[1,128,1024]{2,1,0:T(8,128)(2,1)} %states_hbm.1) | copy-start | bytes 786436
  1.6 0.8 %copy-start.1 = (bf16[64,512]{1,0:T(8,128)(2,1)S(1)}, bf16[64,512]{1,0:T(8,128)(2,1)}, u32[]{:S(2)}) copy-start(bf16[64,512]{1,0:T(8,128)(2,1)} %wq.1) | copy-start | bytes 196612
  2.4 0.8 %copy-start.2 = (bf16[64,512]{1,0:T(8,128)(2,1)S(1)}, bf16[64,512]{1,0:T(8,128)(2,1)}, u32[]{:S(2)}) copy-start(bf16[64,512]{1,0:T(8,128)(2,1)} %wk.1) | copy-start | bytes 196612
  3.3 0.8 %copy-start.3 = (bf16[64,512]{1,0:T(8,128)(2,1)S(1)}, bf16[64,512]{1,0:T(8,128)(2,1)}, u32[]{:S(2)}) copy-start(bf16[64,512]{1,0:T(8,128)(2,1)} %wv.1) | copy-start | bytes 196612
  4.1 0.8 %copy-start.4 = (bf16[32,1024]{1,0:T(8,128)(2,1)S(1)}, bf16[32,1024]{1,0:T(8,128)(2,1)}, u32[]{:S(2)}) copy-start(bf16[32,1024]{1,0:T(8,128)(2,1)} %wo.1) | copy-start | bytes 196612
  4.9 0.8 %copy-start.5 = (f32[128,128]{1,0:T(8,128)S(1)}, f32[128,128]{1,0:T(8,128)}, u32[]{:S(2)}) copy-start(f32[128,128]{1,0:T(8,128)} %obs_hbm.1) | copy-start | bytes 196612
  5.8 0.7 copy-start.6
  6.5 0.7 copy-start.7
  7.2 0.7 copy-start.8

commit v3 on v2

--- a/solution.py
+++ b/solution.py
@@ -303,7 +303,7 @@
 
     split = members == 2 and near == 2 and pair == 2
     begin_qkv, steps_qkv, finish_qkv = gather(qkv_all, 0, split)
-    begin_wo, steps_wo, finish_wo = gather(wo_all, 1, split)
+    begin_wo, steps_wo, finish_wo = gather(wo_all, 1, False)
     begin_wh, steps_wh, finish_wh = gather(wh_all, 2, False)
 
     begin_qkv()
@@ -323,10 +323,11 @@
         count = count + (local[:, k : k + 1] == column).astype(F32)
     count2 = jnp.concatenate([count, count], axis=0)
 
-    for step in steps_qkv:
+    for n, step in enumerate(steps_qkv):
         step()
-    begin_wo()
-    begin_wh()
+        if n == len(steps_qkv) // 3:
+            begin_wo()
+            begin_wh()
     finish_qkv()
     steps_out = []
     for n, step in enumerate(steps_wo):
@@ -574,7 +575,7 @@
                 jax.ShapeDtypeStruct(wh.shape, F32),
                 jax.ShapeDtypeStruct((1, points, 2 * inner), F32),
             ),
-            in_specs=[pl.BlockSpec(memory_space=pl.ANY)] * 9,
+            in_specs=[pl.BlockSpec(memory_space=pltpu.HBM)] * 9,
             out_specs=(pl.BlockSpec(memory_space=pltpu.VMEM),) * 4,
             scratch_shapes=[
                 vm(states.shape, BF),

time: 82.1 us -> 78.6 us (0.957)
  Pallas kernels: 71 us -> 67.4 us
    pallas_call x1, Pallas kernels: 71 us -> 67.4 us  [shards(): pl.pallas_call(functools.partial(kernel, members, grid), out_shape=(jax.S...]
where the time goes in v3:
time: 78.6 us; the launch traced here: 78.1 us
  Pallas kernels  67.4 us (86%)
  local copies, waits for them, and re-layouts  9.99 us (13%)
    pallas_call x1, Pallas kernels, shards(): pl.pallas_call(functools.partial(kernel, members, grid), out_shape=(jax.S...  67.4 us
    unnamed x22, local copies, waits for them, and re-layouts  9.99 us

profile of v3, /device:TPU:0, one launch (start us, length us, event | category | flops | bytes accessed | tf_op | source)
XLA Modules:
  0.0 78.1 jit_solution(4862391967192024552)
XLA Ops:
  0.6 0.0 copy-start
  0.6 0.9 %copy-done = bf16[1,128,1024]{2,1,0:T(8,128)(2,1)S(1)} copy-done((bf16[1,128,1024]{2,1,0:T(8,128)(2,1)S(1)}, bf16[1,128,1024]{2,1,0:T(8,128)(2,1)}, u32[]{:S(2)}) %copy-start) | copy-done | bytes 262168
  1.6 0.0 copy-start.1
  1.6 0.8 %copy-done.1 = bf16[64,512]{1,0:T(8,128)(2,1)S(1)} copy-done((bf16[64,512]{1,0:T(8,128)(2,1)S(1)}, bf16[64,512]{1,0:T(8,128)(2,1)}, u32[]{:S(2)}) %copy-start.1) | copy-done | bytes 65560
  2.4 0.0 copy-start.2
  2.4 0.8 %copy-done.2 = bf16[64,512]{1,0:T(8,128)(2,1)S(1)} copy-done((bf16[64,512]{1,0:T(8,128)(2,1)S(1)}, bf16[64,512]{1,0:T(8,128)(2,1)}, u32[]{:S(2)}) %copy-start.2) | copy-done | bytes 65560
  3.3 0.0 copy-start.3
  3.3 0.8 %copy-done.3 = bf16[64,512]{1,0:T(8,128)(2,1)S(1)} copy-done((bf16[64,512]{1,0:T(8,128)(2,1)S(1)}, bf16[64,512]{1,0:T(8,128)(2,1)}, u32[]{:S(2)}) %copy-start.3) | copy-done | bytes 65560
  4.1 0.0 copy-start.4
  4.1 0.8 %copy-done.4 = bf16[32,1024]{1,0:T(8,128)(2,1)S(1)} copy-done((bf16[32,1024]{1,0:T(8,128)(2,1)S(1)}, bf16[32,1024]{1,0:T(8,128)(2,1)}, u32[]{:S(2)}) %copy-start.4) | copy-done | bytes 65560
  4.9 0.0 copy-start.5
  4.9 0.8 %copy-done.5 = f32[128,128]{1,0:T(8,128)S(1)} copy-done((f32[128,128]{1,0:T(8,128)S(1)}, f32[128,128]{1,0:T(8,128)}, u32[]{:S(2)}) %copy-start.5) | copy-done | bytes 65560
  5.8 0.0 copy-start.6
  5.8 0.7 copy-done.6
  6.5 0.0 copy-start.7
  6.5 0.7 copy-done.7
  7.2 0.0 copy-start.8
  7.2 0.7 copy-done.8
  7.9 67.4 %shard_map.120 = (bf16[1,128,1024]{2,1,0:T(8,128)(2,1)S(1)}, f32[32,1024]{1,0:T(8,128)S(1)}, f32[64,128]{1,0:T(8,128)S(1)}, f32[1,128,1024]{2,1,0:T(8,128)S(1)}) custom-call(bf16[1,128,1024]{2,1,0:T(8,128)(2,1)S(1)} %copy-done, f32[1,1024]{1,0:T(1,128)S(1)} %bitcast.2, bf16[64,512]{1,0:T(8,128)(2,1)S(1)} %copy-done.1, bf16[64,512]{1,0:T(8,128)(2,1)S(1)} %copy-done.2, ...), custom_call_target="tpu_custom_call" | custom-call | tf_op jit(solution)/shard_map/pallas_call | solution.py:570
  75.3 0.7 copy.17
  76.0 0.7 copy.18
  76.7 0.6 copy.19
  77.3 0.8 %copy.20 = f32[1,128,1024]{2,1,0:T(8,128)} copy(f32[1,128,1024]{2,1,0:T(8,128)S(1)} %get-tuple-element.11) | data formatting | bytes 1048576
Async XLA Ops:
  0.6 1.0 %copy-start = (bf16[1,128,1024]{2,1,0:T(8,128)(2,1)S(1)}, bf16[1,128,1024]{2,1,0:T(8,128)(2,1)}, u32[]{:S(2)}) copy-start(bf16[1,128,1024]{2,1,0:T(8,128)(2,1)} %states_hbm.1) | copy-start | bytes 786436
  1.6 0.8 %copy-start.1 = (bf16[64,512]{1,0:T(8,128)(2,1)S(1)}, bf16[64,512]{1,0:T(8,128)(2,1)}, u32[]{:S(2)}) copy-start(bf16[64,512]{1,0:T(8,128)(2,1)} %wq.1) | copy-start | bytes 196612
  2.4 0.8 %copy-start.2 = (bf16[64,512]{1,0:T(8,128)(2,1)S(1)}, bf16[64,512]{1,0:T(8,128)(2,1)}, u32[]{:S(2)}) copy-start(bf16[64,512]{1,0:T(8,128)(2,1)} %wk.1) | copy-start | bytes 196612
  3.3 0.8 %copy-start.3 = (bf16[64,512]{1,0:T(8,128)(2,1)S(1)}, bf16[64,512]{1,0:T(8,128)(2,1)}, u32[]{:S(2)}) copy-start(bf16[64,512]{1,0:T(8,128)(2,1)} %wv.1) | copy-start | bytes 196612
  4.1 0.8 %copy-start.4 = (bf16[32,1024]{1,0:T(8,128)(2,1)S(1)}, bf16[32,1024]{1,0:T(8,128)(2,1)}, u32[]{:S(2)}) copy-start(bf16[32,1024]{1,0:T(8,128)(2,1)} %wo.1) | copy-start | bytes 196612
  4.9 0.8 %copy-start.5 = (f32[128,128]{1,0:T(8,128)S(1)}, f32[128,128]{1,0:T(8,128)}, u32[]{:S(2)}) copy-start(f32[128,128]{1,0:T(8,128)} %obs_hbm.1) | copy-start | bytes 196612
  5.8 0.7 copy-start.6
  6.5 0.7 copy-start.7
  7.2 0.7 copy-start.8
